TPU v7x, 32 devices: a whole 2x2x4 slice. The times are simulated.
32 devices in a mesh: groups: 2 (over y), ctx: 4 (over z), head: 4 (over x, core).
Axes of the slice: x: 2, y: 2, z: 4, core: 2. Of those that a mesh axis runs over, the one named last changes fastest.
Arguments:
- query_rows: bfloat16 [4096, 4096], P(('groups', 'ctx', 'head')), parts along dimension 0, may hold values from -6 to 6
- key_rows: bfloat16 [4096, 4096], P(('groups', 'ctx', 'head')), parts along dimension 0, may hold values from -6 to 6
- value_rows: bfloat16 [4096, 8192], P(('groups', 'ctx', 'head')), parts along dimension 0, may hold values from -30 to 30
- gate_rows: bfloat16 [4096, 8192], P(('groups', 'ctx', 'head')), parts along dimension 0, may hold values from -6 to 6
- decay_log: bfloat16 [4096, 16], P(('groups', 'ctx', 'head')), parts along dimension 0, may hold values from -1 to 0, as said below
- norm_gain: float32 [8192], P('head'), may hold values from 0.25 to 1.75
Outputs:
- retention_out: bfloat16 [4096, 8192], P(('groups', 'ctx', 'head')), parts along dimension 0
There are 2 independent parts, one for each index of `groups`. A program takes and returns all parts, laid end to end along the dimension named above; an argument that names none is the same for every part. Nothing has to cross between parts.
Inputs may be any that keep to these rules, and one draw needn't show every extreme that they name: `decay_log`: every entry is negative.
All inputs are finite; a program needn't handle non-finite values.
Results may differ from a plain program's by a relative error of at most 0.0085.
Values may be sent and summed in bfloat16 or wider, within the bound.
A program may use at most 128 MiB of HBM per device.

v0:
```python
import jax
import jax.numpy as jnp
from jax import lax
from jax.sharding import PartitionSpec as P

KEY_DIM = 256
VALUE_DIM = 512


def prefix(x, axis, combine, identity):
    devices, index = (lax.axis_size(axis), lax.axis_index(axis))
    everything = jax.tree.map(lambda part: lax.all_gather(part, axis), x)
    start = jax.tree.map(
        lambda part, zero: jnp.broadcast_to(jnp.asarray(zero, part.dtype), part.shape), x, identity
    )

    def turn(k, before):
        reached = k < index
        new = combine(before, jax.tree.map(lambda part: part[k], everything))
        return jax.tree.map(lambda a, b: jnp.where(reached, a, b), new, before)

    return lax.fori_loop(0, devices, turn, start)


def merge_states(earlier, latter):
    return (earlier[0] + latter[0], jnp.exp(latter[0])[:, None, None] * earlier[1] + latter[1])


def split_parts(matrix):
    upper = matrix.astype(jnp.bfloat16)
    rest = matrix - lax.optimization_barrier(upper).astype(jnp.float32)
    middle = rest.astype(jnp.bfloat16)
    lowest = (rest - lax.optimization_barrier(middle).astype(jnp.float32)).astype(jnp.bfloat16)
    return (upper, middle, lowest)


def body(query_rows, key_rows, value_rows, gate_rows, decay_log, norm_gain):
    query_heads, key_heads, value_heads, gate_heads, decay_heads = (
        lax.all_to_all(query_rows, "head", split_axis=1, concat_axis=0, tiled=True),
        lax.all_to_all(key_rows, "head", split_axis=1, concat_axis=0, tiled=True),
        lax.all_to_all(value_rows, "head", split_axis=1, concat_axis=0, tiled=True),
        lax.all_to_all(gate_rows, "head", split_axis=1, concat_axis=0, tiled=True),
        lax.all_to_all(decay_log, "head", split_axis=1, concat_axis=0, tiled=True),
    )
    length = query_heads.shape[0]
    local_heads = decay_heads.shape[1]
    query_heads = query_heads.reshape(length, local_heads, KEY_DIM)
    key_heads = key_heads.reshape(length, local_heads, KEY_DIM)
    value_heads = value_heads.reshape(length, local_heads, VALUE_DIM)
    key_scale = KEY_DIM ** (-0.5)
    within = jnp.cumsum(decay_heads.astype(jnp.float32), axis=0)
    block_total = within[-1]
    decayed = (
        key_heads.astype(jnp.float32) * jnp.exp(block_total[None, :] - within)[:, :, None]
    ).astype(jnp.bfloat16)
    block_state = jnp.einsum(
        "jhk,jhd->hkd", decayed, value_heads, preferred_element_type=jnp.float32
    )
    identity = (jnp.zeros_like(block_total), jnp.zeros_like(block_state))
    carried = prefix((block_total, block_state), "ctx", merge_states, identity)[1]
    log_gaps = within.T[:, :, None] - within.T[:, None, :]
    causal = (jnp.arange(length)[:, None] >= jnp.arange(length)[None, :])[None]
    damping = jnp.where(causal, jnp.exp(jnp.where(causal, log_gaps, 0.0)), 0.0)
    scores = jnp.einsum("ihk,jhk->hij", query_heads, key_heads, preferred_element_type=jnp.float32)
    weights = (scores * key_scale * damping).astype(jnp.bfloat16)
    local_out = jnp.einsum("hij,jhd->ihd", weights, value_heads, preferred_element_type=jnp.float32)
    upper, middle, lowest = split_parts(carried)
    inter = jnp.einsum("ihk,hkd->ihd", query_heads, upper, preferred_element_type=jnp.float32)
    inter = inter + jnp.einsum(
        "ihk,hkd->ihd", query_heads, middle, preferred_element_type=jnp.float32
    )
    inter = inter + jnp.einsum(
        "ihk,hkd->ihd", query_heads, lowest, preferred_element_type=jnp.float32
    )
    retained = local_out + inter * (jnp.exp(within) * key_scale)[:, :, None]
    centered = retained - jnp.mean(retained, axis=-1, keepdims=True)
    spread = jnp.mean(centered * centered, axis=-1, keepdims=True)
    normed = (
        centered * lax.rsqrt(spread + 1e-06) * norm_gain.reshape(local_heads, VALUE_DIM)
    ).astype(jnp.bfloat16)
    normed = normed.reshape(length, local_heads * VALUE_DIM)
    mixed = (normed.astype(jnp.float32) * jax.nn.silu(gate_heads.astype(jnp.float32))).astype(
        jnp.bfloat16
    )
    return lax.all_to_all(mixed, "head", split_axis=0, concat_axis=1, tiled=True)


def solution(mesh):
    placed = (
        P(("groups", "ctx", "head"), None),
        P(("groups", "ctx", "head"), None),
        P(("groups", "ctx", "head"), None),
        P(("groups", "ctx", "head"), None),
        P(("groups", "ctx", "head"), None),
        P("head"),
    )
    return jax.shard_map(
        body,
        mesh=mesh,
        in_specs=placed,
        out_specs=P(("groups", "ctx", "head"), None),
        check_vma=False,
    )
```

profile of v0, /device:TPU:0, one launch (start us, length us, event | category | flops | bytes accessed | tf_op | source)
XLA Modules:
  0.0 293.8 jit_solution(11106510641096637045)
XLA Ops:
  6.5 4.2 %all-to-all-start.2 = ((bf16[128,4,4]{0,2,1:T(4,128)(2,1)}), bf16[128,4,4]{0,2,1:T(4,128)(2,1)S(1)}, u32[]{:S(2)}, u32[]{:S(2)}) async-start(bf16[128,4,4]{0,2,1:T(4,128)(2,1)} %bitcast.92), calls=%async_computation.2 | async-start | bytes 8192 | tf_op jit(solution)/shard_map/all_to_all | solution.py:43
  14.5 3.5 %all-to-all-start.1 = ((bf16[128,4,1024]{2,0,1:T(8,128)(2,1)}), bf16[128,4,1024]{2,0,1:T(8,128)(2,1)S(1)}, u32[]{:S(2)}, u32[]{:S(2)}) async-start(bf16[128,4,1024]{2,0,1:T(8,128)(2,1)} %copy.92), calls=%async_computation.1 | async-start | bytes 2097152 | tf_op jit(solution)/shard_map/all_to_all | solution.py:40
  18.1 4.1 %copy.95 = bf16[128,8192]{0,1:T(8,128)(2,1)} copy(bf16[128,8192]{1,0:T(8,128)(2,1)} %param.10) | data formatting | bytes 4194304 | tf_op args[2]
  22.1 10.4 %all-to-all-done.1 = bf16[128,4,1024]{2,0,1:T(8,128)(2,1)S(1)} async-done(((bf16[128,4,1024]{2,0,1:T(8,128)(2,1)}), bf16[128,4,1024]{2,0,1:T(8,128)(2,1)S(1)}, u32[]{:S(2)}, u32[]{:S(2)}) %all-to-all-start.1) | async-done | bytes 1048608 | tf_op jit(solution)/shard_map/all_to_all | solution.py:40
  32.5 3.6 %all-to-all-start.3 = ((bf16[128,4,2048]{0,2,1:T(8,128)(2,1)}), bf16[128,4,2048]{0,2,1:T(8,128)(2,1)S(1)}, u32[]{:S(2)}, u32[]{:S(2)}) async-start(bf16[128,4,2048]{0,2,1:T(8,128)(2,1)} %bitcast.7), calls=%async_computation.3 | async-start | bytes 4194304 | tf_op jit(solution)/shard_map/all_to_all | solution.py:41
  41.6 20.2 %all-to-all-done.3 = bf16[128,4,2048]{0,2,1:T(8,128)(2,1)S(1)} async-done(((bf16[128,4,2048]{0,2,1:T(8,128)(2,1)}), bf16[128,4,2048]{0,2,1:T(8,128)(2,1)S(1)}, u32[]{:S(2)}, u32[]{:S(2)}) %all-to-all-start.3) | async-done | bytes 2097184 | tf_op jit(solution)/shard_map/all_to_all | solution.py:41
  61.8 10.7 %copy.96 = bf16[4,128,2048]{1,0,2:T(4,128)(2,1)} copy(bf16[4,128,2048]{1,2,0:T(8,128)(2,1)S(1)} %bitcast.81) | data formatting | bytes 4194304 | tf_op jit(solution)/shard_map/all_to_all | solution.py:41
  72.5 2.7 reshape.107
  79.7 3.5 %all-to-all-start = ((bf16[128,4,1024]{2,0,1:T(8,128)(2,1)}), bf16[128,4,1024]{2,0,1:T(8,128)(2,1)S(1)}, u32[]{:S(2)}, u32[]{:S(2)}) async-start(bf16[128,4,1024]{2,0,1:T(8,128)(2,1)} %bitcast.85), calls=%async_computation | async-start | bytes 2097152 | tf_op jit(solution)/shard_map/all_to_all | solution.py:39
  83.3 4.1 %copy.106 = bf16[128,8192]{0,1:T(8,128)(2,1)} copy(bf16[128,8192]{1,0:T(8,128)(2,1)} %param.11) | data formatting | bytes 4194304 | tf_op args[3]
  87.5 11.8 %all-gather.1 = f32[4,1,4]{2,1,0:T(1,128)S(1)} all-gather(f32[1,1,4]{2,1,0:T(1,128)S(1)} %bitcast.91), channel_id=1, replica_groups=mesh['groups'=2,'ctx'=4,'head'=4] {'ctx'}, dimensions={0}, use_global_device_ids=true | all-gather | bytes 80 | tf_op jit(solution)/shard_map/all_gather | solution.py:12
  99.3 4.7 %all-to-all-start.4 = ((bf16[128,4,2048]{0,2,1:T(8,128)(2,1)}), bf16[128,4,2048]{0,2,1:T(8,128)(2,1)}, u32[]{:S(2)}, u32[]{:S(2)}) async-start(bf16[128,4,2048]{0,2,1:T(8,128)(2,1)} %bitcast.80), calls=%async_computation.4 | async-start | bytes 4194304 | tf_op jit(solution)/shard_map/all_to_all | solution.py:42
  105.8 6.6 %fusion.8 = f32[4,512,512]{1,2,0:T(8,128)} fusion(bf16[512,4,512]{0,2,1:T(8,128)(2,1)} %copy-done, f32[4,512]{1,0:T(4,128)S(1)} %bitcast.89, pred[512,512]{1,0:T(8,128)(4,1)S(1)} %iota_compare_fusion, bf16[512,4,256]{2,1,0:T(4,128)(2,1)} %reshape.104, bf16[512,4,256]{2,1,0:T(4,128)(2,1)S(1)} %reshape.103), kind=kOutput, calls=%fused_computation.19 | convolution fusion | flops 1616904192 | bytes 8658944 | tf_op jit(solution)/shard_map/hij,jhd->ihd/dot_general | solution.py:66
  112.4 115.5 %all-gather.4.cloned.1.call-done = f32[16,256,512]{2,1,0:T(8,128)} async-done(((f32[4,256,512]{2,1,0:T(8,128)}), f32[16,256,512]{2,1,0:T(8,128)}) %all-gather.4.cloned.1.call-update) | async-done | bytes 8388624 | tf_op jit(solution)/shard_map/all_gather | solution.py:12
  227.9 10.7 %while.14 = (s32[]{:T(128)}, f32[4,256,512]{2,1,0:T(8,128)S(1)}, s32[]{:T(128)}, f32[4,4]{1,0:T(4,128)S(1)}, f32[4,4,256,512]{3,2,1,0:T(8,128)}, /*index=5*/s32[]{:T(128)}, s32[]{:T(128)}) while((s32[]{:T(128)}, f32[4,256,512]{2,1,0:T(8,128)S(1)}, s32[]{:T(128)}, f32[4,4]{1,0:T(4,128)S(1)}, f32[4,4,256,512]{3,2,1,0:T(8,128)}, ...), condition=%wide.region_3.4_spmd.clone, body=%wide.region_2.3_spmd.clone.sunk | while | flops 2097156 | bytes 6291617 | solution.py:22
  227.9 2.6 fusion.30
  230.6 2.6 fusion.30
  233.3 2.6 fusion.30
  235.9 2.6 fusion.30
  244.2 2.5 fusion.7
  246.7 5.2 %reshape.109 = f32[4,128,2048]{1,0,2:T(4,128)} reshape(f32[512,4,512]{0,2,1:T(8,128)} %fusion.7) | data formatting | bytes 8388608 | tf_op jit(solution)/shard_map/convert_element_type | solution.py:82
  251.9 3.9 %fusion.6 = bf16[4,128,2048]{1,2,0:T(8,128)(2,1)S(1)} fusion(bf16[128,4,2048]{0,2,1:T(8,128)(2,1)} %all-to-all-done.4, f32[4,128,2048]{1,0,2:T(4,128)} %reshape.109), kind=kLoop, calls=%fused_computation.14 | loop fusion | flops 7340032 | bytes 8388608 | tf_op jit(solution)/shard_map/convert_element_type | solution.py:82
  255.8 28.3 %all_to_all.90 = bf16[4,128,2048]{1,2,0:T(8,128)(2,1)S(1)} all-to-all(bf16[4,128,2048]{1,2,0:T(8,128)(2,1)S(1)} %fusion.6), channel_id=1, replica_groups=mesh['groups'=2,'ctx'=4,'head'=4] {'head'}, dimensions={0} | all-to-all | bytes 4194304 | tf_op jit(solution)/shard_map/all_to_all | solution.py:85
  284.1 2.9 copy.108
  (45 shorter events, 21.3 us)
Async XLA Ops:
  6.5 8.0 %all-to-all-start.2 = ((bf16[128,4,4]{0,2,1:T(4,128)(2,1)}), bf16[128,4,4]{0,2,1:T(4,128)(2,1)S(1)}, u32[]{:S(2)}, u32[]{:S(2)}) async-start(bf16[128,4,4]{0,2,1:T(4,128)(2,1)} %bitcast.92), calls=%async_computation.2 | async-start | bytes 8192 | tf_op jit(solution)/shard_map/all_to_all | solution.py:43
  14.5 18.0 %all-to-all-start.1 = ((bf16[128,4,1024]{2,0,1:T(8,128)(2,1)}), bf16[128,4,1024]{2,0,1:T(8,128)(2,1)S(1)}, u32[]{:S(2)}, u32[]{:S(2)}) async-start(bf16[128,4,1024]{2,0,1:T(8,128)(2,1)} %copy.92), calls=%async_computation.1 | async-start | bytes 2097152 | tf_op jit(solution)/shard_map/all_to_all | solution.py:40
  32.5 29.3 %all-to-all-start.3 = ((bf16[128,4,2048]{0,2,1:T(8,128)(2,1)}), bf16[128,4,2048]{0,2,1:T(8,128)(2,1)S(1)}, u32[]{:S(2)}, u32[]{:S(2)}) async-start(bf16[128,4,2048]{0,2,1:T(8,128)(2,1)} %bitcast.7), calls=%async_computation.3 | async-start | bytes 4194304 | tf_op jit(solution)/shard_map/all_to_all | solution.py:41
  36.1 191.8 %all-gather.4.cloned.1.call-start = ((), (), s32[]{:S(2)}) async-start(), calls=%async_computation.6 | async-start | bytes 10485760 | tf_op jit(solution)/shard_map/all_gather | solution.py:12
  75.2 4.5 %copy-start = (bf16[512,4,512]{0,2,1:T(8,128)(2,1)}, bf16[512,4,512]{0,2,1:T(8,128)(2,1)S(1)}, u32[]{:S(2)}) copy-start(bf16[512,4,512]{0,2,1:T(8,128)(2,1)S(1)} %reshape.107) | copy-start | bytes 6291460
  77.3 5.9 %copy-start.3 = (f32[2048]{0:T(1024)S(1)}, f32[2048]{0:T(1024)}, u32[]{:S(2)}) copy-start(f32[2048]{0:T(1024)} %param.13) | copy-start | bytes 24580
  79.7 19.6 %all-to-all-start = ((bf16[128,4,1024]{2,0,1:T(8,128)(2,1)}), bf16[128,4,1024]{2,0,1:T(8,128)(2,1)S(1)}, u32[]{:S(2)}, u32[]{:S(2)}) async-start(bf16[128,4,1024]{2,0,1:T(8,128)(2,1)} %bitcast.85), calls=%async_computation | async-start | bytes 2097152 | tf_op jit(solution)/shard_map/all_to_all | solution.py:39
  99.3 4.7 %copy-start.1 = (bf16[128,4,1024]{2,0,1:T(8,128)(2,1)}, bf16[128,4,1024]{2,0,1:T(8,128)(2,1)S(1)}, u32[]{:S(2)}) copy-start(bf16[128,4,1024]{2,0,1:T(8,128)(2,1)S(1)} %all-to-all-done) | copy-start | bytes 3145732
  99.3 152.6 %all-to-all-start.4 = ((bf16[128,4,2048]{0,2,1:T(8,128)(2,1)}), bf16[128,4,2048]{0,2,1:T(8,128)(2,1)}, u32[]{:S(2)}, u32[]{:S(2)}) async-start(bf16[128,4,2048]{0,2,1:T(8,128)(2,1)} %bitcast.80), calls=%async_computation.4 | async-start | bytes 4194304 | tf_op jit(solution)/shard_map/all_to_all | solution.py:42
  239.9 2.2 copy-start.2
Sparse Core Ops, SparseCore 0:
  77.5 150.3 all-gather.3
where the time goes:
time: 295 us; the launch traced here: 294 us
  waiting for transfers between devices  147 us (50%)
  local copies, waits for them, and re-layouts  40.4 us (14%)
  blocking collectives  40.1 us (14%)
  other arithmetic  21.4 us (7%)
  starting transfers between devices  19.5 us (7%)
  between operations  13.6 us (5%)
  matrix products  11.8 us (4%)
    all_gather x1, waiting for transfers between devices, prefix(): everything = jax.tree.map(lambda part: lax.all_gather(part, axis), x)  116 us
    all_to_all x1, blocking collectives, body(): lax.all_to_all(mixed, 'head', split_axis=0, concat_axis=1, tiled=True)  28.3 us
    all_to_all x1, waiting for transfers between devices, body(): lax.all_to_all(value_rows, 'head', split_axis=1, concat_axis=0, tiled=True)  20.2 us
    all_gather x1, blocking collectives, prefix(): everything = jax.tree.map(lambda part: lax.all_gather(part, axis), x)  11.8 us
    unnamed x12, local copies, waits for them, and re-layouts  11.1 us
    all_to_all x1, local copies, waits for them, and re-layouts, body(): lax.all_to_all(value_rows, 'head', split_axis=1, concat_axis=0, tiled=True)  10.7 us
    select_n x4, other arithmetic, turn(): return jax.tree.map(lambda a, b: jnp.where(reached, a, b), new, before)  10.5 us
    all_to_all x1, waiting for transfers between devices, body(): lax.all_to_all(key_rows, 'head', split_axis=1, concat_axis=0, tiled=True)  10.4 us
  transfers between devices with their start and end apart: 6, of which 4 were waited for; matrix products, arithmetic and copies ran while one was open for 17% of the time, Pallas kernels for 0%

commit v1 on v0

--- a/solution.py
+++ b/solution.py
@@ -82,7 +82,10 @@
     mixed = (normed.astype(jnp.float32) * jax.nn.silu(gate_heads.astype(jnp.float32))).astype(
         jnp.bfloat16
     )
-    return lax.all_to_all(mixed, "head", split_axis=0, concat_axis=1, tiled=True)
+    return jnp.concatenate(
+        lax.all_to_all(jnp.stack(jnp.split(mixed, lax.axis_size("head"), axis=0)), "head", 0, 0),
+        axis=1,
+    )
 
 
 def solution(mesh):

time: 295 us -> 288 us (0.976)
  waiting for transfers between devices: 147 us -> 135 us
  local copies, waits for them, and re-layouts: 40.4 us -> 43.6 us
    all_gather x1, waiting for transfers between devices: 116 us -> 83.1 us  [prefix(): everything = jax.tree.map(lambda part: lax.all_gather(part, axis), x)]
    all_to_all x1, waiting for transfers between devices: 0.01 us -> 10.8 us  [body(): lax.all_to_all(gate_rows, 'head', split_axis=1, concat_axis=0, tiled=True)]
    all_to_all x1, waiting for transfers between devices: 0.01 us -> 8.51 us  [body(): lax.all_to_all(query_rows, 'head', split_axis=1, concat_axis=0, tiled=True)]
    unnamed x12 -> x18, local copies, waits for them, and re-layouts: 11.1 us -> 12.5 us
  transfers between devices with their start and end apart: 6 -> 6, of which waited for: 4 -> 6; matrix products, arithmetic and copies ran while one was open for 17% -> 12% of each run, Pallas kernels for 0% -> 0%
where the time goes in v1:
time: 288 us; the launch traced here: 287 us
  waiting for transfers between devices  135 us (47%)
  local copies, waits for them, and re-layouts  43.6 us (15%)
  blocking collectives  41.2 us (14%)
  other arithmetic  21.6 us (8%)
  starting transfers between devices  19.4 us (7%)
  between operations  13.6 us (5%)
  matrix products  11.8 us (4%)
    all_gather x1, waiting for transfers between devices, prefix(): everything = jax.tree.map(lambda part: lax.all_gather(part, axis), x)  83.1 us
    all_to_all x1, blocking collectives, body(): lax.all_to_all(jnp.stack(jnp.split(mixed, lax.axis_size('head'), axis=0))...  28.2 us
    all_to_all x1, waiting for transfers between devices, body(): lax.all_to_all(value_rows, 'head', split_axis=1, concat_axis=0, tiled=True)  20.2 us
    all_gather x1, blocking collectives, prefix(): everything = jax.tree.map(lambda part: lax.all_gather(part, axis), x)  12.9 us
    unnamed x18, local copies, waits for them, and re-layouts  12.5 us
    all_to_all x1, waiting for transfers between devices, body(): lax.all_to_all(key_rows, 'head', split_axis=1, concat_axis=0, tiled=True)  12 us
    all_to_all x1, waiting for transfers between devices, body(): lax.all_to_all(gate_rows, 'head', split_axis=1, concat_axis=0, tiled=True)  10.8 us
    all_to_all x1, local copies, waits for them, and re-layouts, body(): lax.all_to_all(value_rows, 'head', split_axis=1, concat_axis=0, tiled=True)  10.7 us
  transfers between devices with their start and end apart: 6, of which 6 were waited for; matrix products, arithmetic and copies ran while one was open for 12% of the time, Pallas kernels for 0%

profile of v1, /device:TPU:0, one launch (start us, length us, event | category | flops | bytes accessed | tf_op | source)
XLA Modules:
  0.0 286.8 jit_solution(1258153117129009388)
XLA Ops:
  6.5 4.2 %all-to-all-start.2 = ((bf16[128,4,4]{0,2,1:T(4,128)(2,1)}), bf16[128,4,4]{0,2,1:T(4,128)(2,1)S(1)}, u32[]{:S(2)}, u32[]{:S(2)}) async-start(bf16[128,4,4]{0,2,1:T(4,128)(2,1)} %bitcast.89), calls=%async_computation.2 | async-start | bytes 8192 | tf_op jit(solution)/shard_map/all_to_all | solution.py:43
  14.5 3.5 %all-to-all-start.1 = ((bf16[128,4,1024]{2,0,1:T(8,128)(2,1)}), bf16[128,4,1024]{2,0,1:T(8,128)(2,1)S(1)}, u32[]{:S(2)}, u32[]{:S(2)}) async-start(bf16[128,4,1024]{2,0,1:T(8,128)(2,1)} %copy.96), calls=%async_computation.1 | async-start | bytes 2097152 | tf_op jit(solution)/shard_map/all_to_all | solution.py:40
  20.5 12.0 %all-to-all-done.1 = bf16[128,4,1024]{2,0,1:T(8,128)(2,1)S(1)} async-done(((bf16[128,4,1024]{2,0,1:T(8,128)(2,1)}), bf16[128,4,1024]{2,0,1:T(8,128)(2,1)S(1)}, u32[]{:S(2)}, u32[]{:S(2)}) %all-to-all-start.1) | async-done | bytes 1048608 | tf_op jit(solution)/shard_map/all_to_all | solution.py:40
  32.5 3.6 %all-to-all-start.3 = ((bf16[128,4,2048]{0,2,1:T(8,128)(2,1)}), bf16[128,4,2048]{0,2,1:T(8,128)(2,1)S(1)}, u32[]{:S(2)}, u32[]{:S(2)}) async-start(bf16[128,4,2048]{0,2,1:T(8,128)(2,1)} %bitcast.7), calls=%async_computation.3 | async-start | bytes 4194304 | tf_op jit(solution)/shard_map/all_to_all | solution.py:41
  41.6 20.2 %all-to-all-done.3 = bf16[128,4,2048]{0,2,1:T(8,128)(2,1)S(1)} async-done(((bf16[128,4,2048]{0,2,1:T(8,128)(2,1)}), bf16[128,4,2048]{0,2,1:T(8,128)(2,1)S(1)}, u32[]{:S(2)}, u32[]{:S(2)}) %all-to-all-start.3) | async-done | bytes 2097184 | tf_op jit(solution)/shard_map/all_to_all | solution.py:41
  61.8 10.7 %copy.100 = bf16[4,128,2048]{1,0,2:T(4,128)(2,1)} copy(bf16[4,128,2048]{1,2,0:T(8,128)(2,1)S(1)} %bitcast.78) | data formatting | bytes 4194304 | tf_op jit(solution)/shard_map/all_to_all | solution.py:41
  72.5 2.7 reshape.111
  79.7 3.5 %all-to-all-start = ((bf16[128,4,1024]{2,0,1:T(8,128)(2,1)}), bf16[128,4,1024]{2,0,1:T(8,128)(2,1)S(1)}, u32[]{:S(2)}, u32[]{:S(2)}) async-start(bf16[128,4,1024]{2,0,1:T(8,128)(2,1)} %bitcast.68), calls=%async_computation | async-start | bytes 2097152 | tf_op jit(solution)/shard_map/all_to_all | solution.py:39
  83.3 3.3 %copy.110 = bf16[128,8192]{0,1:T(8,128)(2,1)S(1)} copy(bf16[128,8192]{1,0:T(8,128)(2,1)} %param.11) | data formatting | bytes 4194304 | tf_op args[3]
  89.2 8.5 %all-to-all-done = bf16[128,4,1024]{2,0,1:T(8,128)(2,1)S(1)} async-done(((bf16[128,4,1024]{2,0,1:T(8,128)(2,1)}), bf16[128,4,1024]{2,0,1:T(8,128)(2,1)S(1)}, u32[]{:S(2)}, u32[]{:S(2)}) %all-to-all-start) | async-done | bytes 1048608 | tf_op jit(solution)/shard_map/all_to_all | solution.py:39
  98.7 4.5 %all-to-all-start.4 = ((bf16[128,4,2048]{2,0,1:T(8,128)(2,1)}), bf16[128,4,2048]{2,0,1:T(8,128)(2,1)}, u32[]{:S(2)}, u32[]{:S(2)}) async-start(bf16[128,4,2048]{2,0,1:T(8,128)(2,1)} %copy.111), calls=%async_computation.4 | async-start | bytes 4194304 | tf_op jit(solution)/shard_map/all_to_all | solution.py:42
  103.3 12.9 %all-gather.1 = f32[4,1,4]{2,1,0:T(1,128)S(1)} all-gather(f32[1,1,4]{2,1,0:T(1,128)S(1)} %bitcast.88), channel_id=1, replica_groups=mesh['groups'=2,'ctx'=4,'head'=4] {'ctx'}, dimensions={0}, use_global_device_ids=true | all-gather | bytes 80 | tf_op jit(solution)/shard_map/all_gather | solution.py:12
  118.1 10.8 %all-to-all-done.4 = bf16[128,4,2048]{2,0,1:T(8,128)(2,1)} async-done(((bf16[128,4,2048]{2,0,1:T(8,128)(2,1)}), bf16[128,4,2048]{2,0,1:T(8,128)(2,1)}, u32[]{:S(2)}, u32[]{:S(2)}) %all-to-all-start.4) | async-done | bytes 2097184 | tf_op jit(solution)/shard_map/all_to_all | solution.py:42
  128.9 4.1 %convert_element_type.71 = f32[128,4,2048]{2,0,1:T(8,128)} convert(bf16[128,4,2048]{2,0,1:T(8,128)(2,1)} %all-to-all-done.4) | non-fusion elementwise | flops 1048576 | bytes 6291456 | tf_op jit(solution)/shard_map/convert_element_type | solution.py:82
  133.0 5.4 %copy.113 = f32[512,2048]{0,1:T(8,128)} copy(f32[512,2048]{1,0:T(8,128)} %bitcast.76) | data formatting | bytes 8388608 | tf_op jit(solution)/shard_map/convert_element_type | solution.py:82
  138.4 6.5 %fusion.3 = f32[4,512,512]{1,2,0:T(8,128)} fusion(bf16[512,4,512]{0,2,1:T(8,128)(2,1)} %copy-done.1, f32[4,512]{1,0:T(4,128)S(1)} %bitcast.86, pred[512,512]{1,0:T(8,128)(4,1)S(1)} %iota_compare_fusion, bf16[512,4,256]{2,1,0:T(4,128)(2,1)} %reshape.108, bf16[512,4,256]{2,1,0:T(4,128)(2,1)S(1)} %reshape.107), kind=kOutput, calls=%fused_computation.14 | convolution fusion | flops 1616904192 | bytes 8658944 | tf_op jit(solution)/shard_map/hij,jhd->ihd/dot_general | solution.py:66
  144.9 83.1 %all-gather.4.cloned.1.call-done = f32[16,256,512]{2,1,0:T(8,128)} async-done(((f32[4,256,512]{2,1,0:T(8,128)}), f32[16,256,512]{2,1,0:T(8,128)}) %all-gather.4.cloned.1.call-update) | async-done | bytes 8388624 | tf_op jit(solution)/shard_map/all_gather | solution.py:12
  228.0 10.6 %while.14 = (s32[]{:T(128)}, f32[4,256,512]{2,1,0:T(8,128)S(1)}, s32[]{:T(128)}, f32[4,4]{1,0:T(4,128)S(1)}, f32[4,4,256,512]{3,2,1,0:T(8,128)}, /*index=5*/s32[]{:T(128)}, s32[]{:T(128)}) while((s32[]{:T(128)}, f32[4,256,512]{2,1,0:T(8,128)S(1)}, s32[]{:T(128)}, f32[4,4]{1,0:T(4,128)S(1)}, f32[4,4,256,512]{3,2,1,0:T(8,128)}, ...), condition=%wide.region_3.4_spmd.clone, body=%wide.region_2.3_spmd.clone.sunk | while | flops 2097156 | bytes 6291609 | solution.py:22
  228.0 2.6 fusion.25
  230.7 2.6 fusion.25
  233.3 2.6 fusion.25
  236.0 2.6 fusion.25
  248.8 28.2 %all_to_all.79 = bf16[4,128,2048]{1,2,0:T(8,128)(2,1)S(1)} all-to-all(bf16[4,128,2048]{1,2,0:T(8,128)(2,1)S(1)} %pad_maximum_fusion), channel_id=1, replica_groups=mesh['groups'=2,'ctx'=4,'head'=4] {'head'}, dimensions={0} | all-to-all | bytes 4194304 | tf_op jit(solution)/shard_map/all_to_all | solution.py:86
  277.0 2.9 %copy.119 = bf16[128,8192]{1,0:T(8,128)(2,1)} copy(bf16[128,8192]{0,1:T(8,128)(2,1)S(1)} %bitcast.79) | data formatting | bytes 4194304 | tf_op jit(solution)/shard_map/reshape | solution.py:85
  (55 shorter events, 31.8 us)
Async XLA Ops:
  6.5 8.0 %all-to-all-start.2 = ((bf16[128,4,4]{0,2,1:T(4,128)(2,1)}), bf16[128,4,4]{0,2,1:T(4,128)(2,1)S(1)}, u32[]{:S(2)}, u32[]{:S(2)}) async-start(bf16[128,4,4]{0,2,1:T(4,128)(2,1)} %bitcast.89), calls=%async_computation.2 | async-start | bytes 8192 | tf_op jit(solution)/shard_map/all_to_all | solution.py:43
  13.7 4.4 %copy-start.4 = (bf16[128,8192]{1,0:T(8,128)(2,1)S(1)}, bf16[128,8192]{1,0:T(8,128)(2,1)}, u32[]{:S(2)}) copy-start(bf16[128,8192]{1,0:T(8,128)(2,1)} %param.10) | copy-start | bytes 6291460
  14.5 18.0 %all-to-all-start.1 = ((bf16[128,4,1024]{2,0,1:T(8,128)(2,1)}), bf16[128,4,1024]{2,0,1:T(8,128)(2,1)S(1)}, u32[]{:S(2)}, u32[]{:S(2)}) async-start(bf16[128,4,1024]{2,0,1:T(8,128)(2,1)} %copy.96), calls=%async_computation.1 | async-start | bytes 2097152 | tf_op jit(solution)/shard_map/all_to_all | solution.py:40
  32.5 29.3 %all-to-all-start.3 = ((bf16[128,4,2048]{0,2,1:T(8,128)(2,1)}), bf16[128,4,2048]{0,2,1:T(8,128)(2,1)S(1)}, u32[]{:S(2)}, u32[]{:S(2)}) async-start(bf16[128,4,2048]{0,2,1:T(8,128)(2,1)} %bitcast.7), calls=%async_computation.3 | async-start | bytes 4194304 | tf_op jit(solution)/shard_map/all_to_all | solution.py:41
  36.1 191.9 %all-gather.4.cloned.1.call-start = ((), (), s32[]{:S(2)}) async-start(), calls=%async_computation.6 | async-start | bytes 10485760 | tf_op jit(solution)/shard_map/all_gather | solution.py:12
  75.2 2.2 copy-start.1
  77.4 1.2 copy-start.5
  79.7 18.0 %all-to-all-start = ((bf16[128,4,1024]{2,0,1:T(8,128)(2,1)}), bf16[128,4,1024]{2,0,1:T(8,128)(2,1)S(1)}, u32[]{:S(2)}, u32[]{:S(2)}) async-start(bf16[128,4,1024]{2,0,1:T(8,128)(2,1)} %bitcast.68), calls=%async_computation | async-start | bytes 2097152 | tf_op jit(solution)/shard_map/all_to_all | solution.py:39
  89.2 14.0 %copy-start.6 = (f32[2048]{0:T(1024)S(1)}, f32[2048]{0:T(1024)}, u32[]{:S(2)}) copy-start(f32[2048]{0:T(1024)} %param.13) | copy-start | bytes 24580
  97.7 1.0 copy-start.2
  98.7 30.3 %all-to-all-start.4 = ((bf16[128,4,2048]{2,0,1:T(8,128)(2,1)}), bf16[128,4,2048]{2,0,1:T(8,128)(2,1)}, u32[]{:S(2)}, u32[]{:S(2)}) async-start(bf16[128,4,2048]{2,0,1:T(8,128)(2,1)} %copy.111), calls=%async_computation.4 | async-start | bytes 4194304 | tf_op jit(solution)/shard_map/all_to_all | solution.py:42
  240.0 2.2 copy-start.3
  244.2 2.2 copy-start
Sparse Core Ops, SparseCore 0:
  77.5 150.4 all-gather.3
